TPU v7x, 256 devices: a whole 4x4x8 slice. The times are simulated.
256 devices in a mesh: head: 2 (over x_lo), inner: 16 (over y, x_hi, core), outer: 8 (over z).
Axes of the slice: x: 4 (x_hi: 2, x_lo: 2; x = x_hi * 2 + x_lo), y: 4, z: 8, core: 2. Of those that a mesh axis runs over, the one named last changes fastest.
Arguments:
- query: bfloat16 [16384, 1792], P(('head', 'inner', 'outer')), may hold values from -12.5 to 12.5
- key: bfloat16 [16384, 256], P(('head', 'inner', 'outer')), may hold values from -2.5 to 2.5
- value: bfloat16 [16384, 256], P(('head', 'inner', 'outer')), may hold values from -6 to 6
- grad_out: bfloat16 [16384, 1792], P(('head', 'inner', 'outer')), may hold values from -288 to 288
Outputs:
- grad_query: bfloat16 [16384, 1792], P(('head', 'inner', 'outer'))
- grad_key: bfloat16 [16384, 256], P(('head', 'inner', 'outer'))
- grad_value: bfloat16 [16384, 256], P(('head', 'inner', 'outer'))
All inputs are finite; a program needn't handle non-finite values.
Results may differ from a plain program's by a relative error of at most 0.02.
Values may be sent and summed in bfloat16 or wider, within the bound.
A program may use at most 64 MiB of HBM per device.

v0:
```python
import functools
import math

import jax
import jax.numpy as jnp
from jax import lax
from jax.experimental import pallas as pl
from jax.experimental.pallas import tpu as pltpu
from jax.sharding import PartitionSpec as P

HQ = 14
HK = 2
DH = 128
ROWS = 64
GROUP = HQ // HK
NX = 4
NY = 4
NZ = 4
PAIR = 2 * GROUP * ROWS
QROWS = 2 * PAIR
BLOCK = NZ * 2 * ROWS
HALF = 2 * 2 * ROWS
SCALE = 1.0 / math.sqrt(DH)
SCALE2 = SCALE * math.log2(math.e)
F32 = jnp.float32
BF16 = jnp.bfloat16


def dot(left, right, left_dim, right_dim):
    return lax.dot_general(
        left, right, (((left_dim,), (right_dim,)), ((), ())), preferred_element_type=F32
    )


def kernel(
    q_in, k_in, v_in, g_in, dq_out, dk_out, dv_out,
    q_buf, k_buf, v_buf, g_buf,
    qg_stage, kv_stage, qg_all, kv_all, e_ref, mb_ref, m_ref, l_ref, d_ref, m_other, l_other, d_other, lse_ref, mean_ref,
    dq_acc, terms, dkv, core_rx, y_sum, y_rx, z_sum, z_rx, dq_stage, dq_rx,
    in_sem, qg_send, qg_recv, z_send, piece_recv, y_send, f_send, chunk_recv, c_send, c_recv,
    stat_send, stat_recv, dc_send, dc_recv, dy_send, dy_recv, dz_send, dz_recv,
    dq_send, dq_recv,
):
    xl = lax.axis_index("head")
    inner = lax.axis_index("inner")
    outer = lax.axis_index("outer")
    y = inner // 4
    xh = (inner // 2) % 2
    c = inner % 2
    zs = outer % NZ
    z0 = outer - zs
    zq = zs // 2

    def at_x(pair, other):
        return {"inner": 4 * y + 2 * other + c, "head": (xl + 1 - pair) % 2}

    def at_y(step):
        other = (y + step) % NY
        return other, {"inner": 4 * other + 2 * xh + c}

    def at_z(step):
        other = (zs + step) % NZ
        return other, {"outer": z0 + other}

    at_core = {"inner": 4 * y + 2 * xh + 1 - c}
    at_swap = {"head": 1 - xl}
    at_half = {"inner": 4 * y + 2 * (1 - xh) + c}

    def remote(src, dst, send_sem, recv_sem, device):
        return pltpu.make_async_remote_copy(
            src_ref=src, dst_ref=dst, send_sem=send_sem, recv_sem=recv_sem,
            device_id=device, device_id_type=pl.DeviceIdType.MESH,
        )

    barrier = pltpu.get_barrier_semaphore()
    x_partners = [(0, xh), (0, 1 - xh), (1, 1 - xh)]
    partners = [at_x(*place) for place in x_partners]
    partners += [at(step)[1] for at in (at_y, at_z) for step in (1, 2, 3)] + [at_core]
    partners += [{**at_z(step)[1], **at_swap} for step in (1, 2, 3)]
    for device in partners:
        pl.semaphore_signal(barrier, inc=1, device_id=device, device_id_type=pl.DeviceIdType.MESH)

    loads = [
        pltpu.make_async_copy(src, dst, in_sem.at[place])
        for place, (src, dst) in enumerate(
            [(k_in, k_buf), (v_in, v_buf), (q_in, q_buf), (g_in, g_buf)]
        )
    ]
    for load in loads:
        load.start()
    mine = pl.ds(pl.multiple_of(xl * DH, DH), DH)
    theirs = pl.ds(pl.multiple_of((1 - xl) * DH, DH), DH)
    loads[0].wait()
    kv_stage[0] = k_buf[:, theirs]
    kv_all[y, c, zs, xl, 0] = k_buf[:, mine]
    loads[1].wait()
    kv_stage[1] = v_buf[:, theirs]
    kv_all[y, c, zs, xl, 1] = v_buf[:, mine]
    pl.semaphore_wait(barrier, len(partners))

    sends = []

    def begin(copy):
        copy.start()
        sends.append(copy)

    def piece_copy(src, zpos, part, send_sem, device):
        return remote(src, kv_all.at[y, c, zpos, part], send_sem, piece_recv.at[zpos, part], device)

    swap = piece_copy(kv_stage, zs, xl, z_send.at[0, 0], at_swap)
    swap.start()
    for step in (1, 3, 2):
        begin(piece_copy(kv_all.at[y, c, zs, xl], zs, xl, z_send.at[step, 0], at_z(step)[1]))

    def query_copy(place):
        pair, other = x_partners[place]
        return remote(
            qg_stage.at[(xl + 1 - pair) % 2], qg_all.at[:, pair, xh], qg_send.at[place],
            qg_recv.at[pair, xh], at_x(pair, other),
        )

    def wait_queries(place):
        pair, other = x_partners[place]
        remote(
            qg_stage.at[0], qg_all.at[:, pair, other], qg_send.at[place], qg_recv.at[pair, other],
            at_x(pair, other),
        ).wait_recv()

    loads[2].wait()
    loads[3].wait()
    for head in range(HQ):
        columns = pl.ds(head * DH, DH)
        qg_stage[head // GROUP, 0, head % GROUP] = q_buf[:, columns]
        qg_stage[head // GROUP, 1, head % GROUP] = g_buf[:, columns]
    begin(query_copy(0))
    begin(query_copy(1))
    qg_all[:, 1, xh] = qg_stage[xl]

    def chunk_copy(ypos, zpos, send_sem, device):
        place = kv_all.at[ypos, c, zpos]
        return remote(place, place, send_sem, chunk_recv.at[ypos, zpos], device)

    def block_copy(ypos, core):
        place = kv_all.at[ypos, core]
        return remote(place, place, c_send.at[ypos], c_recv.at[ypos, core], at_core)

    def forward_copy(step):
        ystep, target = (1, 3) if step < 2 else (3, 1)
        return chunk_copy(
            (y + ystep) % NY, (zs + step) % NZ, f_send.at[step], at_y(target)[1]
        )

    piece_copy(kv_stage, zs, 1 - xl, z_send.at[0, 0], at_swap).wait_recv()
    for step in (1, 3, 2):
        place = kv_all.at[y, c, zs, 1 - xl]
        begin(piece_copy(place, zs, 1 - xl, z_send.at[step, 1], at_z(step)[1]))
    for step in (0, 1, 3, 2):
        zpos, device = at_z(step)
        if step:
            for part in (xl, 1 - xl):
                piece_copy(kv_stage, zpos, part, z_send.at[0, 0], device).wait_recv()
        for place, ystep in enumerate((1, 3)):
            begin(chunk_copy(y, zpos, y_send.at[place, step], at_y(ystep)[1]))
        if step == 0:
            begin(query_copy(2))
    begin(block_copy(y, c))

    def wait_chunk(ystep, step):
        ypos, device = at_y(ystep)
        chunk_copy(ypos, (zs + step) % NZ, y_send.at[0, 0], device).wait_recv()

    for step in (0, 1, 3, 2):
        for ystep in (1, 3):
            wait_chunk(ystep, step)
            if (step < 2) == (ystep == 1):
                begin(forward_copy(step))
    for ystep in (1, 3):
        begin(block_copy((y + ystep) % NY, c))
    for place in range(3):
        wait_queries(place)

    queries = qg_all.at[0].reshape(QROWS, DH)
    out_grads = qg_all.at[1].reshape(QROWS, DH)

    stats = [(m_ref, m_other), (l_ref, l_other), (d_ref, d_other)]

    def stat_copy(kind):
        own, other = stats[kind]
        return remote(own, other, stat_send.at[kind], stat_recv.at[kind], at_half)

    def wait_core(ystep):
        block_copy((y + ystep) % NY, 1 - c).wait_recv()

    m_ref[...] = jnp.full_like(m_ref, -1e30)
    l_ref[...] = jnp.zeros_like(l_ref)
    d_ref[...] = jnp.zeros_like(d_ref)

    def stats_step(turn, carry):
        @pl.when(turn == 1)
        def first():
            wait_core(0)

        @pl.when(turn == 3)
        def second():
            wait_core(1)

        @pl.when(turn == 4)
        def opposite():
            for step in range(NZ):
                wait_chunk(2, step)
            block_copy((y + 2) % NY, c).start()

        @pl.when(turn == 5)
        def third():
            wait_core(3)

        @pl.when(turn == 7)
        def last():
            wait_core(2)

        slot, role = turn // 2, turn % 2
        ypos = (y + slot + slot // 2 - 2 * (slot // 3)) % NY
        core = c + role * (1 - 2 * c)
        keys = kv_all[ypos, core, :, :, 0].reshape(BLOCK, DH)
        values = kv_all[ypos, core, :, :, 1].reshape(BLOCK, DH)
        scores = dot(keys, queries[...], 1, 1)
        prob_grad = dot(values, out_grads[...], 1, 1)
        old = m_ref[...]
        new = jnp.maximum(old, jnp.max(scores, axis=0, keepdims=True) * SCALE2)
        factor = jnp.exp2(old - new)
        weights = jnp.exp2(scores * SCALE2 - new)
        e_ref[ypos, core] = weights.astype(BF16)
        mb_ref[ypos, core] = new
        m_ref[...] = new
        l_ref[...] = l_ref[...] * factor + jnp.sum(weights, axis=0, keepdims=True)
        d_ref[...] = d_ref[...] * factor + jnp.sum(weights * prob_grad, axis=0, keepdims=True)
        return carry

    lax.fori_loop(0, 2 * NY, stats_step, 0)

    for kind in range(3):
        stat_copy(kind).start()
    dq_acc[...] = jnp.zeros_like(dq_acc)
    for kind in range(3):
        stat_copy(kind).wait_recv()
    top = jnp.maximum(m_ref[...], m_other[...])
    own_factor = jnp.exp2(m_ref[...] - top)
    other_factor = jnp.exp2(m_other[...] - top)
    total = l_ref[...] * own_factor + l_other[...] * other_factor
    weighted = d_ref[...] * own_factor + d_other[...] * other_factor
    lse_ref[...] = top + jnp.log2(total)
    mean_ref[...] = weighted / total

    def grad_block(ypos, half):
        keys = kv_all[ypos, :, pl.ds(2 * half, 2), :, 0].reshape(2 * HALF, DH)
        values = kv_all[ypos, :, pl.ds(2 * half, 2), :, 1].reshape(2 * HALF, DH)
        prob_grad = dot(values, out_grads[...], 1, 1)
        place = pl.ds(pl.multiple_of(half * HALF, HALF), HALF)
        probs = jnp.concatenate(
            [
                e_ref[ypos, core, place, :].astype(F32)
                * jnp.exp2(mb_ref[ypos, core] - lse_ref[...])
                for core in range(2)
            ],
            axis=0,
        )
        grad_low = (probs * (prob_grad - mean_ref[...])).astype(BF16)
        value_term = dot(probs.astype(BF16), out_grads[...], 1, 0)
        key_term = dot(grad_low, queries[...], 1, 0) * SCALE
        dq_acc[...] += dot(keys, grad_low, 0, 0)
        shape = (2, 2, 2, ROWS, DH)
        return key_term.reshape(shape), value_term.reshape(shape)

    def core_copy(ypos, half):
        place = pl.ds(2 * half, 2)
        return remote(
            dkv.at[ypos, place], core_rx.at[ypos, place], dc_send.at[ypos, half],
            dc_recv.at[ypos, half], at_core,
        )

    def y_copy(ypos, sender, half, device):
        place = pl.ds(2 * half, 2)
        return remote(
            y_sum.at[ypos, place], y_rx.at[sender, place], dy_send.at[ypos, half],
            dy_recv.at[sender, half], device,
        )

    def y_total(half):
        place = pl.ds(2 * half, 2)
        for step in (1, 2, 3):
            ypos, device = at_y(step)
            y_copy(ypos, ypos, half, device).wait_recv()
        total = y_sum[y, place].astype(F32)
        for step in (1, 2, 3):
            total = total + y_rx[(y + step) % NY, place].astype(F32)
        z_sum[place] = total.astype(BF16)

    def z_copy(zpos, part, place):
        return remote(
            z_sum.at[zpos, part], z_rx.at[zs, xl], dz_send.at[place], dz_recv.at[zs, xl],
            {"outer": z0 + zpos, "head": part},
        )

    def wait_z(zpos, part):
        remote(
            z_sum.at[zpos, part], z_rx.at[zpos, part], dz_send.at[0], dz_recv.at[zpos, part],
            {"outer": z0 + zpos, "head": part},
        ).wait_recv()

    far_places = [(2 * (1 - zq) + place // 2, place % 2, place) for place in range(4)]
    near = 4 * zq + 1 - zs
    near_places = [(near, 0, 4), (near, 1, 5), (zs, 1 - xl, 6)]

    def grad_place(turn):
        late, slot = turn % 2, turn // 2
        half = (1 - late) * (1 - zq) + late * zq
        ystep = ((1 - slot // 2) * (2 - slot) + slot // 2 * (slot + 1)) % NY
        return half, slot, at_y(ystep)

    def put_other(turn):
        half, slot, (ypos, device) = grad_place(turn)
        for kind in range(2):
            dkv[ypos, pl.ds(2 * half, 2), :, kind] = terms[turn % 2, kind, 1 - c].astype(BF16)
        core_copy(ypos, half).start()

    def put_own(turn):
        half, slot, (ypos, device) = grad_place(turn)
        place = pl.ds(2 * half, 2)
        core_copy(ypos, half).wait_recv()
        for kind in range(2):
            total = terms[turn % 2, kind, c] + core_rx[ypos, place, :, kind].astype(F32)
            y_sum[ypos, place, :, kind] = total.astype(BF16)

        @pl.when(slot < NY - 1)
        def send():
            y_copy(ypos, y, half, device).start()

    def grad_step(turn, carry):
        half, slot, (ypos, device) = grad_place(turn)
        for kind, term in enumerate(grad_block(ypos, half)):
            terms[turn % 2, kind] = term
        put_other(turn)

        @pl.when(turn > 0)
        def last_turn():
            put_own(turn - 1)

        return carry

    lax.fori_loop(0, 2 * NY, grad_step, 0)
    y_total(1 - zq)
    for far in far_places:
        z_copy(*far).start()

    for pair in (1, 0):
        done = (dq_acc[:, pl.ds(pair * PAIR, PAIR)] * SCALE).T.astype(BF16)
        dq_stage[pair] = done.reshape(2, GROUP, ROWS, DH)
        for place, (of_pair, other) in enumerate(x_partners):
            if of_pair == pair:
                begin(
                    remote(
                        dq_stage.at[pair, other], dq_rx.at[pair, xh], dq_send.at[place],
                        dq_recv.at[pair, xh], at_x(pair, other),
                    )
                )
    dq_rx[1, xh] = dq_stage[1, xh]
    put_own(2 * NY - 1)
    y_total(zq)
    for near_place in near_places:
        z_copy(*near_place).start()
    z_rx[zs, xl] = z_sum[zs, xl]
    for step in (2, 3, 1):
        for part in range(2):
            wait_z(at_z(step)[0], part)
    wait_z(zs, 1 - xl)
    for head in range(HK):
        total = z_rx[0, head].astype(F32)
        for zpos in range(1, NZ):
            total = total + z_rx[zpos, head].astype(F32)
        dk_out[:, pl.ds(head * DH, DH)] = total[0].astype(BF16)
        dv_out[:, pl.ds(head * DH, DH)] = total[1].astype(BF16)

    for pair, other in x_partners:
        remote(
            dq_stage.at[0, 0], dq_rx.at[pair, other], dq_send.at[0], dq_recv.at[pair, other],
            at_x(pair, other),
        ).wait_recv()
    for head in range(HQ):
        group, place = head // GROUP, head % GROUP
        pair = (xl + group + 1) % 2
        both = dq_rx[pair, 0, place].astype(F32) + dq_rx[pair, 1, place].astype(F32)
        dq_out[:, pl.ds(head * DH, DH)] = both.astype(BF16)

    for copy in sends:
        copy.wait_send()
    swap.wait_send()
    for kind in range(3):
        stat_copy(kind).wait_send()
    block_copy((y + 2) % NY, c).wait_send()
    for place in far_places + near_places:
        z_copy(*place).wait_send()
    for half in range(2):
        for ypos in range(NY):
            core_copy(ypos, half).wait_send()
        for step in (1, 2, 3):
            ypos, device = at_y(step)
            y_copy(ypos, y, half, device).wait_send()


def on_device(query, key, value, grad_out):
    vmem = pl.BlockSpec(memory_space=pltpu.VMEM)
    dma = pltpu.SemaphoreType.DMA
    rows = query.shape[0]
    return pl.pallas_call(
        kernel,
        out_shape=(
            pltpu.VMEM(query.shape, BF16),
            pltpu.VMEM(key.shape, BF16),
            pltpu.VMEM(value.shape, BF16),
        ),
        in_specs=[pl.BlockSpec(memory_space=pl.ANY)] * 4,
        out_specs=(vmem,) * 3,
        scratch_shapes=[
            pltpu.VMEM((rows, HQ * DH), BF16),
            pltpu.VMEM((rows, HK * DH), BF16),
            pltpu.VMEM((rows, HK * DH), BF16),
            pltpu.VMEM((rows, HQ * DH), BF16),
            pltpu.VMEM((HK, 2, GROUP, ROWS, DH), BF16),
            pltpu.VMEM((2, ROWS, DH), BF16),
            pltpu.VMEM((2, 2, 2, GROUP, ROWS, DH), BF16),
            pltpu.VMEM((NY, 2, NZ, 2, 2, ROWS, DH), BF16),
            pltpu.VMEM((NY, 2, BLOCK, QROWS), BF16),
            pltpu.VMEM((NY, 2, 1, QROWS), F32),
            pltpu.VMEM((1, QROWS), F32),
            pltpu.VMEM((1, QROWS), F32),
            pltpu.VMEM((1, QROWS), F32),
            pltpu.VMEM((1, QROWS), F32),
            pltpu.VMEM((1, QROWS), F32),
            pltpu.VMEM((1, QROWS), F32),
            pltpu.VMEM((1, QROWS), F32),
            pltpu.VMEM((1, QROWS), F32),
            pltpu.VMEM((DH, QROWS), F32),
            pltpu.VMEM((2, 2, 2, 2, 2, ROWS, DH), F32),
            pltpu.VMEM((NY, NZ, 2, 2, ROWS, DH), BF16),
            pltpu.VMEM((NY, NZ, 2, 2, ROWS, DH), BF16),
            pltpu.VMEM((NY, NZ, 2, 2, ROWS, DH), BF16),
            pltpu.VMEM((NY, NZ, 2, 2, ROWS, DH), BF16),
            pltpu.VMEM((NZ, 2, 2, ROWS, DH), BF16),
            pltpu.VMEM((NZ, 2, 2, ROWS, DH), BF16),
            pltpu.VMEM((2, 2, GROUP, ROWS, DH), BF16),
            pltpu.VMEM((2, 2, GROUP, ROWS, DH), BF16),
            dma((4,)),
            dma((3,)),
            dma((2, 2)),
            dma((NZ, 2)),
            dma((NZ, 2)),
            dma((2, NZ)),
            dma((NZ,)),
            dma((NY, NZ)),
            dma((NY,)),
            dma((NY, 2)),
            dma((3,)),
            dma((3,)),
            dma((NY, 2)),
            dma((NY, 2)),
            dma((NY, 2)),
            dma((NY, 2)),
            dma((7,)),
            dma((NZ, 2)),
            dma((3,)),
            dma((2, 2)),
        ],
        compiler_params=pltpu.CompilerParams(
            collective_id=0, has_side_effects=True, vmem_limit_bytes=60 * 2**20
        ),
    )(query, key, value, grad_out)

def solution(mesh):
    spec = P(("head", "inner", "outer"), None)
    return jax.shard_map(
        on_device, mesh=mesh, in_specs=(spec,) * 4, out_specs=(spec,) * 3, check_vma=False
    )
```

profile of v0, /device:TPU:2, one launch (start us, length us, event | category | flops | bytes accessed | tf_op | source)
XLA Modules:
  0.0 63.8 jit_solution(3475243525592472978)
XLA Ops:
  0.6 61.3 %shard_map.67 = (bf16[64,1792]{1,0:T(8,128)(2,1)S(1)}, bf16[64,256]{1,0:T(8,128)(2,1)S(1)}, bf16[64,256]{1,0:T(8,128)(2,1)S(1)}) custom-call(bf16[64,1792]{1,0:T(8,128)(2,1)} %q_in.1, bf16[64,256]{1,0:T(8,128)(2,1)} %k_in.1, bf16[64,256]{1,0:T(8,128)(2,1)} %v_in.1, bf16[64,1792]{1,0:T(8,128)(2,1)} %g_in.1), custom_call_target="tpu_custom_call" | custom-call | tf_op jit(solution)/shard_map/pallas_call | solution.py:414
  61.9 0.7 %copy.10 = bf16[64,1792]{1,0:T(8,128)(2,1)} copy(bf16[64,1792]{1,0:T(8,128)(2,1)S(1)} %get-tuple-element.3) | data formatting | bytes 458752
  62.6 0.6 copy.11
  63.2 0.6 copy.12
where the time goes:
time: 63.9 us; the launch traced here: 63.8 us
  Pallas kernels  61.3 us (96%)
  local copies, waits for them, and re-layouts  1.92 us (3%)
  between operations  0.64 us (1%)
    pallas_call x1, Pallas kernels, on_device(): pl.pallas_call(kernel, out_shape=(pltpu.VMEM(query.shape, BF16), pltpu.VM...  61.3 us
    unnamed x3, local copies, waits for them, and re-layouts  1.92 us

commit v1 on v0

--- a/solution.py
+++ b/solution.py
@@ -18,7 +18,7 @@
 NZ = 4
 PAIR = 2 * GROUP * ROWS
 QROWS = 2 * PAIR
-BLOCK = NZ * 2 * ROWS
+BLOCK = 2 * NZ * 2 * ROWS
 HALF = 2 * 2 * ROWS
 SCALE = 1.0 / math.sqrt(DH)
 SCALE2 = SCALE * math.log2(math.e)
@@ -197,46 +197,38 @@
 
     def stats_step(turn, carry):
         @pl.when(turn == 1)
-        def first():
-            wait_core(0)
-
-        @pl.when(turn == 3)
         def second():
             wait_core(1)
 
-        @pl.when(turn == 4)
-        def opposite():
+        @pl.when(turn == 2)
+        def third():
             for step in range(NZ):
                 wait_chunk(2, step)
             block_copy((y + 2) % NY, c).start()
-
-        @pl.when(turn == 5)
-        def third():
             wait_core(3)
 
-        @pl.when(turn == 7)
+        @pl.when(turn == 3)
         def last():
             wait_core(2)
 
-        slot, role = turn // 2, turn % 2
-        ypos = (y + slot + slot // 2 - 2 * (slot // 3)) % NY
-        core = c + role * (1 - 2 * c)
-        keys = kv_all[ypos, core, :, :, 0].reshape(BLOCK, DH)
-        values = kv_all[ypos, core, :, :, 1].reshape(BLOCK, DH)
+        ypos = (y + turn + turn // 2 - 2 * (turn // 3)) % NY
+        keys = kv_all[ypos, :, :, :, 0].reshape(BLOCK, DH)
+        values = kv_all[ypos, :, :, :, 1].reshape(BLOCK, DH)
         scores = dot(keys, queries[...], 1, 1)
         prob_grad = dot(values, out_grads[...], 1, 1)
         old = m_ref[...]
         new = jnp.maximum(old, jnp.max(scores, axis=0, keepdims=True) * SCALE2)
         factor = jnp.exp2(old - new)
         weights = jnp.exp2(scores * SCALE2 - new)
-        e_ref[ypos, core] = weights.astype(BF16)
-        mb_ref[ypos, core] = new
+        e_ref[ypos] = weights.astype(BF16).reshape(2, BLOCK // 2, QROWS)
+        mb_ref[ypos] = new
         m_ref[...] = new
         l_ref[...] = l_ref[...] * factor + jnp.sum(weights, axis=0, keepdims=True)
         d_ref[...] = d_ref[...] * factor + jnp.sum(weights * prob_grad, axis=0, keepdims=True)
         return carry
 
-    lax.fori_loop(0, 2 * NY, stats_step, 0)
+    wait_core(0)
+    lax.fori_loop(0, NY, stats_step, 0)
 
     for kind in range(3):
         stat_copy(kind).start()
@@ -256,14 +248,8 @@
         values = kv_all[ypos, :, pl.ds(2 * half, 2), :, 1].reshape(2 * HALF, DH)
         prob_grad = dot(values, out_grads[...], 1, 1)
         place = pl.ds(pl.multiple_of(half * HALF, HALF), HALF)
-        probs = jnp.concatenate(
-            [
-                e_ref[ypos, core, place, :].astype(F32)
-                * jnp.exp2(mb_ref[ypos, core] - lse_ref[...])
-                for core in range(2)
-            ],
-            axis=0,
-        )
+        factor = jnp.exp2(mb_ref[ypos] - lse_ref[...])
+        probs = e_ref[ypos, :, place, :].reshape(2 * HALF, QROWS).astype(F32) * factor
         grad_low = (probs * (prob_grad - mean_ref[...])).astype(BF16)
         value_term = dot(probs.astype(BF16), out_grads[...], 1, 0)
         key_term = dot(grad_low, queries[...], 1, 0) * SCALE
@@ -429,8 +415,8 @@
             pltpu.VMEM((2, ROWS, DH), BF16),
             pltpu.VMEM((2, 2, 2, GROUP, ROWS, DH), BF16),
             pltpu.VMEM((NY, 2, NZ, 2, 2, ROWS, DH), BF16),
-            pltpu.VMEM((NY, 2, BLOCK, QROWS), BF16),
-            pltpu.VMEM((NY, 2, 1, QROWS), F32),
+            pltpu.VMEM((NY, 2, BLOCK // 2, QROWS), BF16),
+            pltpu.VMEM((NY, 1, QROWS), F32),
             pltpu.VMEM((1, QROWS), F32),
             pltpu.VMEM((1, QROWS), F32),
             pltpu.VMEM((1, QROWS), F32),

time: 63.9 us -> 62.8 us (0.983)
  Pallas kernels: 61.3 us -> 60.2 us
    pallas_call x1, Pallas kernels: 61.3 us -> 60.2 us  [on_device(): pl.pallas_call(kernel, out_shape=(pltpu.VMEM(query.shape, BF16), pltpu.VM...]
where the time goes in v1:
time: 62.8 us; the launch traced here: 62.7 us
  Pallas kernels  60.2 us (96%)
  local copies, waits for them, and re-layouts  1.92 us (3%)
  between operations  0.64 us (1%)
    pallas_call x1, Pallas kernels, on_device(): pl.pallas_call(kernel, out_shape=(pltpu.VMEM(query.shape, BF16), pltpu.VM...  60.2 us
    unnamed x3, local copies, waits for them, and re-layouts  1.92 us

profile of v1, /device:TPU:2, one launch (start us, length us, event | category | flops | bytes accessed | tf_op | source)
XLA Modules:
  0.0 62.7 jit_solution(6972429806674415426)
XLA Ops:
  0.6 60.2 %shard_map.67 = (bf16[64,1792]{1,0:T(8,128)(2,1)S(1)}, bf16[64,256]{1,0:T(8,128)(2,1)S(1)}, bf16[64,256]{1,0:T(8,128)(2,1)S(1)}) custom-call(bf16[64,1792]{1,0:T(8,128)(2,1)} %q_in.1, bf16[64,256]{1,0:T(8,128)(2,1)} %k_in.1, bf16[64,256]{1,0:T(8,128)(2,1)} %v_in.1, bf16[64,1792]{1,0:T(8,128)(2,1)} %g_in.1), custom_call_target="tpu_custom_call" | custom-call | tf_op jit(solution)/shard_map/pallas_call | solution.py:400
  60.8 0.7 %copy.10 = bf16[64,1792]{1,0:T(8,128)(2,1)} copy(bf16[64,1792]{1,0:T(8,128)(2,1)S(1)} %get-tuple-element.3) | data formatting | bytes 458752
  61.5 0.6 copy.11
  62.1 0.6 copy.12

commit v2 on v1

--- a/solution.py
+++ b/solution.py
@@ -145,7 +145,7 @@
         return remote(place, place, c_send.at[ypos], c_recv.at[ypos, core], at_core)
 
     def forward_copy(step):
-        ystep, target = (1, 3) if step < 2 else (3, 1)
+        ystep, target = (1, 3) if step % 2 == 0 else (3, 1)
         return chunk_copy(
             (y + ystep) % NY, (zs + step) % NZ, f_send.at[step], at_y(target)[1]
         )
@@ -172,7 +172,7 @@
     for step in (0, 1, 3, 2):
         for ystep in (1, 3):
             wait_chunk(ystep, step)
-            if (step < 2) == (ystep == 1):
+            if (step % 2 == 0) == (ystep == 1):
                 begin(forward_copy(step))
     for ystep in (1, 3):
         begin(block_copy((y + ystep) % NY, c))
@@ -334,10 +334,6 @@
         return carry
 
     lax.fori_loop(0, 2 * NY, grad_step, 0)
-    y_total(1 - zq)
-    for far in far_places:
-        z_copy(*far).start()
-
     for pair in (1, 0):
         done = (dq_acc[:, pl.ds(pair * PAIR, PAIR)] * SCALE).T.astype(BF16)
         dq_stage[pair] = done.reshape(2, GROUP, ROWS, DH)
@@ -349,6 +345,9 @@
                         dq_recv.at[pair, xh], at_x(pair, other),
                     )
                 )
+    y_total(1 - zq)
+    for far in far_places:
+        z_copy(*far).start()
     dq_rx[1, xh] = dq_stage[1, xh]
     put_own(2 * NY - 1)
     y_total(zq)

time: 62.8 us -> 63 us (level)
  no operation moved by 1% of the time
where the time goes in v2:
time: 63 us; the launch traced here: 62.9 us
  Pallas kernels  60.3 us (96%)
  local copies, waits for them, and re-layouts  1.92 us (3%)
  between operations  0.64 us (1%)
    pallas_call x1, Pallas kernels, on_device(): pl.pallas_call(kernel, out_shape=(pltpu.VMEM(query.shape, BF16), pltpu.VM...  60.3 us
    unnamed x3, local copies, waits for them, and re-layouts  1.92 us

profile of v2, /device:TPU:2, one launch (start us, length us, event | category | flops | bytes accessed | tf_op | source)
XLA Modules:
  0.0 62.9 jit_solution(585024355474790266)
XLA Ops:
  0.6 60.3 %shard_map.67 = (bf16[64,1792]{1,0:T(8,128)(2,1)S(1)}, bf16[64,256]{1,0:T(8,128)(2,1)S(1)}, bf16[64,256]{1,0:T(8,128)(2,1)S(1)}) custom-call(bf16[64,1792]{1,0:T(8,128)(2,1)} %q_in.1, bf16[64,256]{1,0:T(8,128)(2,1)} %k_in.1, bf16[64,256]{1,0:T(8,128)(2,1)} %v_in.1, bf16[64,1792]{1,0:T(8,128)(2,1)} %g_in.1), custom_call_target="tpu_custom_call" | custom-call | tf_op jit(solution)/shard_map/pallas_call | solution.py:399
  60.9 0.7 %copy.10 = bf16[64,1792]{1,0:T(8,128)(2,1)} copy(bf16[64,1792]{1,0:T(8,128)(2,1)S(1)} %get-tuple-element.3) | data formatting | bytes 458752
  61.6 0.6 copy.11
  62.2 0.6 copy.12
